TPU v7x, 256 devices: a whole 4x4x8 slice. The times are simulated.
256 devices in a mesh: leaf: 8 (over y, core), front: 32 (over z, x).
Axes of the slice: x: 4, y: 4, z: 8, core: 2. Of those that a mesh axis runs over, the one named last changes fastest.
Arguments:
- leaf_inverse: bfloat16 [8192, 128, 128], P(('leaf', 'front')), may hold values from -0.5 to 0.5
- leaf_rhs: bfloat16 [8192, 128, 256], P(('leaf', 'front')), may hold values from -6 to 6
- off_blocks: bfloat16 [8192, 5, 128, 128], P(('leaf', 'front')), may hold values from -0.0546875 to 0.0546875
- block_rows: int32 [8192, 5], P(('leaf', 'front')), may hold values from 0 to 63
- fill_count: int32 [8192], P(('leaf', 'front')), may hold values from 1 to 5
- sep_rhs: bfloat16 [256, 128, 256], P(('leaf', 'front')), may hold values from -6 to 6
- panel_order: int32 [8, 32], P('leaf'), may hold values from 0 to 31, each once within a row
- sep_inverse: bfloat16 [256, 128, 4096], P(('leaf', 'front')), may hold values from -0.09375 to 0.09375
Outputs:
- leaf_solution: bfloat16 [8192, 128, 256], P(('leaf', 'front'))
- sep_forward: bfloat16 [256, 128, 256], P(('leaf', 'front'))
- sep_solution: float32 [256, 128, 256], P(('leaf', 'front'))
Inputs may be any that keep to these rules, and one draw needn't show every extreme that they name: Each row of panel_order is a permutation of the 32 separators of that front.
All inputs are finite; a program needn't handle non-finite values.
Results may differ from a plain program's by a relative error of at most 0.025.
Values may be sent and summed in bfloat16 or wider, within the bound.
No kernel may reach another device: no remote copies, remote signals or barrier semaphores. Data moves between devices by JAX's collectives and lax.ppermute only.
A program may use at most 128 MiB of HBM per device.

v0:
```python
import jax
import jax.numpy as jnp
from jax import lax
from jax.sharding import PartitionSpec as P


def swapped(shard, axis, bit):
    return lax.ppermute(shard, axis, [(i, i ^ 1 << bit) for i in range(lax.axis_size(axis))])


def on_device(
    leaf_inverse, leaf_rhs, off_blocks, block_rows, fill_count, sep_rhs, panel_order, sep_inverse
):
    block_width = leaf_inverse.shape[1]
    probe_count = leaf_rhs.shape[2]
    owned_count = sep_rhs.shape[0]
    fronts = lax.axis_size("front")
    front_seps = owned_count * fronts
    parity = lax.axis_index("leaf") % 2
    forward = jnp.einsum(
        "kab,kbr->kar", leaf_inverse, leaf_rhs, preferred_element_type=jnp.float32
    ).astype(jnp.bfloat16)
    used_slots = jnp.arange(off_blocks.shape[1], dtype=jnp.int32)[None, :] < fill_count[:, None]
    product = jnp.einsum("kpab,kbr->kpar", off_blocks, forward, preferred_element_type=jnp.float32)
    product = jnp.where(used_slots[:, :, None, None], product, jnp.zeros((), jnp.float32))
    product = product.reshape(-1, block_width, probe_count)
    half_index = block_rows // front_seps
    local_index = block_rows % front_seps
    sibling_flag = (half_index != parity).astype(jnp.int32)
    target = (
        local_index // owned_count * (2 * owned_count)
        + sibling_flag * owned_count
        + local_index % owned_count
    )
    partial_terms = (
        jnp.zeros((2 * front_seps, block_width, probe_count), jnp.float32)
        .at[target.reshape(-1)]
        .add(product)
    )
    shares = lax.psum_scatter(
        partial_terms.astype(jnp.bfloat16), "front", scatter_dimension=0, tiled=True
    ).astype(jnp.float32)
    received = swapped(shares[owned_count:].astype(jnp.bfloat16), "leaf", 0).astype(jnp.float32)
    summed = shares[:owned_count] + received
    separator_in = (sep_rhs.astype(jnp.float32) - summed).astype(jnp.bfloat16)
    arrived = lax.all_gather(separator_in, "front", axis=0, tiled=True)
    arrived_rows = arrived.shape[0]
    columns = sep_inverse
    flat = arrived.reshape(arrived_rows * block_width, probe_count)
    forward_sep = jnp.einsum(
        "sac,cr->sar", columns, flat, preferred_element_type=jnp.float32
    ).astype(jnp.bfloat16)
    owned_rows = lax.dynamic_slice_in_dim(
        panel_order[0], lax.axis_index("front") * owned_count, owned_count
    )
    placed = (
        jnp.zeros((front_seps, block_width, probe_count), jnp.float32)
        .at[owned_rows]
        .set(forward_sep.astype(jnp.float32))
    )
    sep_forward = lax.psum_scatter(
        placed.astype(jnp.bfloat16), "front", scatter_dimension=0, tiled=True
    )
    columns = sep_inverse
    result = jnp.einsum("sac,sar->cr", columns, forward_sep, preferred_element_type=jnp.float32)
    sep_solution = lax.psum_scatter(
        result.reshape(owned_count * lax.axis_size("front"), block_width, probe_count).astype(
            jnp.bfloat16
        ),
        "front",
        scatter_dimension=0,
        tiled=True,
    ).astype(jnp.float32)
    solved = sep_solution.astype(jnp.bfloat16)
    whole_front = lax.all_gather(solved, "front", axis=0, tiled=True)
    other_front = swapped(whole_front, "leaf", 0)
    lower_front = jnp.where(parity == 0, whole_front, other_front)
    upper_front = jnp.where(parity == 0, other_front, whole_front)
    pair_field = jnp.concatenate([lower_front, upper_front], axis=0)
    picked = pair_field[block_rows]
    picked = jnp.where(used_slots[:, :, None, None], picked, jnp.zeros((), jnp.bfloat16))
    pulled = jnp.einsum("kpab,kpar->kbr", off_blocks, picked, preferred_element_type=jnp.float32)
    backward = (forward.astype(jnp.float32) - pulled).astype(jnp.bfloat16)
    leaf_solution = jnp.einsum(
        "kba,kbr->kar", leaf_inverse, backward, preferred_element_type=jnp.float32
    ).astype(jnp.bfloat16)
    return (leaf_solution, sep_forward, sep_solution)


def solution(mesh):
    placed = (
        P(("leaf", "front"), None, None),
        P(("leaf", "front"), None, None),
        P(("leaf", "front"), None, None, None),
        P(("leaf", "front"), None),
        P(("leaf", "front")),
        P(("leaf", "front"), None, None),
        P("leaf", None),
        P(("leaf", "front"), None, None),
    )
    return jax.shard_map(
        on_device,
        mesh=mesh,
        in_specs=placed,
        out_specs=(
            P(("leaf", "front"), None, None),
            P(("leaf", "front"), None, None),
            P(("leaf", "front"), None, None),
        ),
        check_vma=False,
    )
```

profile of v0, /device:TPU:8, one launch (start us, length us, event | category | flops | bytes accessed | tf_op | source)
XLA Modules:
  0.0 925.7 jit_solution(462579910879347742)
XLA Ops:
  7.2 0.0 reduce-scatter.4.cloned.1.call-start
  7.2 0.8 add_select_fusion
  8.1 0.1 copy.27
  8.2 0.1 reshape.113
  8.3 0.9 iota_compare_fusion
  9.2 2.1 convolution_convert_fusion
  11.3 9.0 broadcast_select_fusion
  20.3 21.2 %copy.29 = f32[160,128,256]{2,1,0:T(8,128)} copy(f32[160,128,256]{1,2,0:T(8,128)} %bitcast.45) | data formatting | bytes 41943040 | tf_op jit(solution)/shard_map/reshape | solution.py:26
  41.5 4.3 broadcast_in_dim.40
  45.8 48.0 %scatter_fusion = f32[64,128,256]{2,1,0:T(8,128)} fusion(f32[64,128,256]{2,1,0:T(8,128)} %broadcast_in_dim.40, s32[160]{0:T(256)S(1)} %bitcast.50, f32[160,128,256]{2,1,0:T(8,128)} %copy.29), kind=kCustom, calls=%fused_computation.1 | custom fusion | flops 5242880 | bytes 62915200 | tf_op jit(solution)/shard_map/scatter-add | solution.py:38
  93.8 6.0 convert_element_type.59
  99.7 0.0 reduce-scatter.4.cloned.1.call-update
  99.7 0.0 all-gather.3.cloned.1.call-start
  99.8 224.4 %reduce-scatter.4.cloned.1.call-done = bf16[2,128,256]{2,1,0:T(8,128)(2,1)} async-done(((bf16[64,128,256]{2,1,0:T(8,128)(2,1)}), bf16[2,128,256]{2,1,0:T(8,128)(2,1)}) %reduce-scatter.4.cloned.1.call-update) | async-done | bytes 131088 | tf_op jit(solution)/shard_map/reduce_scatter | solution.py:40
  324.2 0.8 slice.35
  325.0 1.3 collective-permute-done
  326.3 1.5 subtract_convert_fusion
  327.8 0.0 all-gather.3.cloned.1.call-update
  327.8 0.0 reduce-scatter.6.cloned.1.call-start
  327.8 0.7 copy.44
  328.5 75.5 %all-gather.3.cloned.1.call-done = bf16[32,128,256]{2,1,0:T(8,128)(2,1)} async-done(((bf16[1,128,256]{2,1,0:T(8,128)(2,1)}), bf16[32,128,256]{2,1,0:T(8,128)(2,1)}) %all-gather.3.cloned.1.call-update) | async-done | bytes 2097168 | tf_op jit(solution)/shard_map/all_gather | solution.py:46
  404.0 2.4 convolution_convert_fusion.1
  406.4 2.0 convert_bitcast_fusion.1
  408.4 0.0 reduce-scatter.6.cloned.1.call-update
  408.5 0.0 all-gather.5.cloned.1.call-start
  408.5 213.6 %reduce-scatter.6.cloned.1.call-done = bf16[1,128,256]{1,2,0:T(8,128)(2,1)} async-done(((bf16[32,128,256]{1,2,0:T(8,128)(2,1)}), bf16[1,128,256]{1,2,0:T(8,128)(2,1)}) %reduce-scatter.6.cloned.1.call-update) | async-done | bytes 65552 | tf_op jit(solution)/shard_map/reduce_scatter | solution.py:66
  622.1 1.6 copy.31
  623.7 0.0 all-gather.5.cloned.1.call-update
  623.8 0.0 reduce-scatter.8.cloned.1.call-start
  623.8 0.6 constant_dynamic-slice_fusion
  626.4 0.7 and_reduce_fusion
  627.1 0.6 select_bitcast_fusion
  627.6 0.1 copy.36
  627.8 0.2 broadcast_in_dim.45
  628.0 1.3 copy-done.2
  629.4 0.0 reduce-scatter.8.cloned.1.call-update
  629.4 72.0 %all-gather.5.cloned.1.call-done = bf16[32,128,256]{2,1,0:T(8,128)(2,1)} async-done(((bf16[1,128,256]{2,1,0:T(8,128)(2,1)}), bf16[32,128,256]{2,1,0:T(8,128)(2,1)}) %all-gather.5.cloned.1.call-update) | async-done | bytes 2097168 | tf_op jit(solution)/shard_map/all_gather | solution.py:75
  701.3 0.1 copy.32
  701.4 0.1 reshape.121
  701.6 0.8 copy.38
  702.3 3.5 collective-permute-done.1
  705.8 2.5 broadcast_select_fusion.2
  708.3 2.4 pad_maximum_fusion
  710.8 9.8 %gather_fusion = bf16[160,128,256]{2,1,0:T(8,128)(2,1)} fusion(bf16[64,128,256]{2,1,0:T(8,128)(2,1)} %pad_maximum_fusion, s32[1024]{0:T(1024)S(1)} %pad_clamp_fusion), kind=kCustom, calls=%fused_computation | custom fusion | bytes 20972160 | tf_op jit(solution)/shard_map/gather | solution.py:80
  720.6 15.1 %copy.33 = bf16[32,5,128,256]{2,3,1,0:T(8,128)(2,1)} copy(bf16[32,5,128,256]{3,2,1,0:T(8,128)(2,1)} %bitcast.46) | data formatting | bytes 20971520 | tf_op jit(solution)/shard_map/gather | solution.py:80
  735.7 9.2 convert_bitcast_fusion
  744.9 4.1 copy.37
  749.0 170.2 %reduce-scatter.8.cloned.1.call-done = bf16[1,128,256]{2,1,0:T(8,128)(2,1)} async-done(((bf16[32,128,256]{2,1,0:T(8,128)(2,1)}), bf16[1,128,256]{2,1,0:T(8,128)(2,1)}) %reduce-scatter.8.cloned.1.call-update) | async-done | bytes 65552 | tf_op jit(solution)/shard_map/reduce_scatter | solution.py:61
  (26 shorter events, 0.1 us)
Async XLA Ops:
  7.2 2.0 copy-start
  7.2 317.0 %reduce-scatter.4.cloned.1.call-start = ((), (), s32[]{:S(2)}) async-start(), calls=%async_computation.3 | async-start | bytes 4325376 | tf_op jit(solution)/shard_map/reduce_scatter | solution.py:40
  8.3 3.0 copy-start.4
  11.3 9.0 copy-start.3
  99.7 226.6 %copy-start.8 = (bf16[1,128,256]{2,1,0:T(8,128)(2,1)S(1)}, bf16[1,128,256]{2,1,0:T(8,128)(2,1)}, u32[]{:S(2)}) copy-start(bf16[1,128,256]{2,1,0:T(8,128)(2,1)} %param.15) | copy-start | bytes 196612
  99.7 228.1 %copy-start.5 = (bf16[1,128,4096]{2,1,0:T(8,128)(2,1)S(1)}, bf16[1,128,4096]{2,1,0:T(8,128)(2,1)}, u32[]{:S(2)}) copy-start(bf16[1,128,4096]{2,1,0:T(8,128)(2,1)} %param.17) | copy-start | bytes 3145732
  99.7 304.3 %all-gather.3.cloned.1.call-start = ((), (), s32[]{:S(2)}) async-start(), calls=%async_computation.4 | async-start | bytes 2162688 | tf_op jit(solution)/shard_map/all_gather | solution.py:46
  325.0 1.3 collective-permute-start
  327.8 294.3 %reduce-scatter.6.cloned.1.call-start = ((), (), s32[]{:S(2)}) async-start(), calls=%async_computation.5 | async-start | bytes 2162688 | tf_op jit(solution)/shard_map/reduce_scatter | solution.py:66
  404.0 219.8 %copy-start.10 = (s32[1,32]{1,0:T(1,128)S(1)}, s32[1,32]{1,0:T(1,128)}, u32[]{:S(2)}) copy-start(s32[1,32]{1,0:T(1,128)} %param.16) | copy-start | bytes 388
  404.0 222.3 %copy-start.9 = (s32[3]{0:T(128)S(1)}, s32[3]{0:T(128)}, u32[]{:S(2)}) copy-start(s32[3]{0:T(128)} %constant.102.clone.1) | copy-start | bytes 40
  408.5 292.9 %all-gather.5.cloned.1.call-start = ((), (), s32[]{:S(2)}) async-start(), calls=%async_computation.6 | async-start | bytes 2162688 | tf_op jit(solution)/shard_map/all_gather | solution.py:75
  622.1 79.5 %copy-start.7 = (bf16[1,128,256]{1,2,0:T(8,128)(2,1)S(1)}, bf16[1,128,256]{1,2,0:T(8,128)(2,1)}, u32[]{:S(2)}) copy-start(bf16[1,128,256]{1,2,0:T(8,128)(2,1)} %reduce-scatter.6.cloned.1.call-done) | copy-start | bytes 196612
  623.8 295.4 %reduce-scatter.8.cloned.1.call-start = ((), (), s32[]{:S(2)}) async-start(), calls=%async_computation.7 | async-start | bytes 2162688 | tf_op jit(solution)/shard_map/reduce_scatter | solution.py:61
  628.0 1.3 copy-start.2
  701.3 4.5 collective-permute-start.1
  720.6 15.1 %copy-start.6 = (bf16[32,128,128]{2,1,0:T(8,128)(2,1)S(1)}, bf16[32,128,128]{2,1,0:T(8,128)(2,1)}, u32[]{:S(2)}) copy-start(bf16[32,128,128]{2,1,0:T(8,128)(2,1)} %param.10) | copy-start | bytes 3145732
  735.7 183.5 %copy-start.1 = (bf16[32,128,256]{2,1,0:T(8,128)(2,1)S(1)}, bf16[32,128,256]{2,1,0:T(8,128)(2,1)}, u32[]{:S(2)}) copy-start(bf16[32,128,256]{2,1,0:T(8,128)(2,1)} %param.11) | copy-start | bytes 6291460
Sparse Core Ops, SparseCore 0:
  99.9 224.2 reduce-scatter.3
  327.9 76.0 all-gather.2
  408.6 213.4 reduce-scatter.5
  625.1 76.2 all-gather.4
  705.6 213.5 reduce-scatter.7
where the time goes:
time: 927 us; the launch traced here: 926 us
  waiting for transfers between devices  760 us (82%)
  other arithmetic  63.3 us (7%)
  local copies, waits for them, and re-layouts  61.1 us (7%)
  matrix products  24.7 us (3%)
  between operations  15.9 us (2%)
    reduce_scatter x1, waiting for transfers between devices, on_device(): lax.psum_scatter(partial_terms.astype(jnp.bfloat16), 'front', scatter_dim...  224 us
    reduce_scatter x1, waiting for transfers between devices, on_device(): lax.psum_scatter(result.reshape(owned_count * lax.axis_size('front'), blo...  214 us
    reduce_scatter x1, waiting for transfers between devices, on_device(): lax.psum_scatter(placed.astype(jnp.bfloat16), 'front', scatter_dimension=...  170 us
    all_gather x1, waiting for transfers between devices, on_device(): arrived = lax.all_gather(separator_in, 'front', axis=0, tiled=True)  75.5 us
    all_gather x1, waiting for transfers between devices, on_device(): whole_front = lax.all_gather(solved, 'front', axis=0, tiled=True)  72 us
    scatter-add x1, other arithmetic, on_device(): partial_terms = jnp.zeros((2 * front_seps, block_width, probe_count), jnp...  48 us
    gather x2, local copies, waits for them, and re-layouts, on_device(): picked = pair_field[block_rows]  24.9 us
    reshape x1, local copies, waits for them, and re-layouts, on_device(): product = product.reshape(-1, block_width, probe_count)  21.2 us
  transfers between devices with their start and end apart: 7, of which 7 were waited for; matrix products, arithmetic and copies ran while one was open for 5% of the time, Pallas kernels for 0%

commit v1 on v0

--- a/solution.py
+++ b/solution.py
@@ -72,7 +72,9 @@
         tiled=True,
     ).astype(jnp.float32)
     solved = sep_solution.astype(jnp.bfloat16)
-    whole_front = lax.all_gather(solved, "front", axis=0, tiled=True)
+    whole_front = jnp.concatenate(
+        lax.all_to_all(jnp.stack([solved] * lax.axis_size("front")), "front", 0, 0), axis=0
+    )
     other_front = swapped(whole_front, "leaf", 0)
     lower_front = jnp.where(parity == 0, whole_front, other_front)
     upper_front = jnp.where(parity == 0, other_front, whole_front)

time: 927 us -> 868 us (0.936)
  waiting for transfers between devices: 760 us -> 694 us
    all_gather x1 -> x0, waiting for transfers between devices: 72 us -> none  [on_device(): whole_front = lax.all_gather(solved, 'front', axis=0, tiled=True)]
    all_to_all x0 -> x1, waiting for transfers between devices: none -> 41.1 us  [on_device(): lax.all_to_all(jnp.stack([solved] * lax.axis_size('front')), 'front', 0, 0)]
    reduce_scatter x1, waiting for transfers between devices: 170 us -> 134 us  [on_device(): lax.psum_scatter(placed.astype(jnp.bfloat16), 'front', scatter_dimension=...]
where the time goes in v1:
time: 868 us; the launch traced here: 867 us
  waiting for transfers between devices  694 us (80%)
  other arithmetic  63.7 us (7%)
  local copies, waits for them, and re-layouts  61.6 us (7%)
  matrix products  24.6 us (3%)
  between operations  15.9 us (2%)
    reduce_scatter x1, waiting for transfers between devices, on_device(): lax.psum_scatter(partial_terms.astype(jnp.bfloat16), 'front', scatter_dim...  224 us
    reduce_scatter x1, waiting for transfers between devices, on_device(): lax.psum_scatter(result.reshape(owned_count * lax.axis_size('front'), blo...  214 us
    reduce_scatter x1, waiting for transfers between devices, on_device(): lax.psum_scatter(placed.astype(jnp.bfloat16), 'front', scatter_dimension=...  134 us
    all_gather x1, waiting for transfers between devices, on_device(): arrived = lax.all_gather(separator_in, 'front', axis=0, tiled=True)  75.5 us
    scatter-add x1, other arithmetic, on_device(): partial_terms = jnp.zeros((2 * front_seps, block_width, probe_count), jnp...  48.2 us
    all_to_all x1, waiting for transfers between devices, on_device(): lax.all_to_all(jnp.stack([solved] * lax.axis_size('front')), 'front', 0, 0)  41.1 us
    gather x2, local copies, waits for them, and re-layouts, on_device(): picked = pair_field[block_rows]  24.6 us
    reshape x1, local copies, waits for them, and re-layouts, on_device(): product = product.reshape(-1, block_width, probe_count)  21.2 us
  transfers between devices with their start and end apart: 7, of which 7 were waited for; matrix products, arithmetic and copies ran while one was open for 5% of the time, Pallas kernels for 0%

profile of v1, /device:TPU:8, one launch (start us, length us, event | category | flops | bytes accessed | tf_op | source)
XLA Modules:
  0.0 866.6 jit_solution(8743753568595279669)
XLA Ops:
  7.2 0.0 reduce-scatter.4.cloned.1.call-start
  7.2 0.8 add_select_fusion
  8.1 0.1 copy.29
  8.2 0.1 reshape.119
  8.3 0.9 iota_compare_fusion
  9.2 2.1 convolution_convert_fusion
  11.3 9.0 %broadcast_select_fusion = f32[32,256,5,128]{3,1,2,0:T(8,128)} fusion(pred[32,5]{1,0:T(8,128)(4,1)S(1)} %iota_compare_fusion, bf16[32,5,128,128]{3,2,1,0:T(8,128)(2,1)S(1)} %copy-done.4, bf16[32,128,256]{2,1,0:T(8,128)(2,1)S(1)} %convolution_convert_fusion), kind=kOutput, calls=%fused_computation.4 | convolution fusion | flops 1347420160 | bytes 28311712 | tf_op jit(solution)/shard_map/kpab,kbr->kpar/dot_general | solution.py:24
  20.3 21.2 %copy.31 = f32[160,128,256]{2,1,0:T(8,128)} copy(f32[160,128,256]{1,2,0:T(8,128)} %bitcast.49) | data formatting | bytes 41943040 | tf_op jit(solution)/shard_map/reshape | solution.py:26
  41.5 4.3 broadcast_in_dim.40
  45.8 48.2 %scatter_fusion = f32[64,128,256]{2,1,0:T(8,128)} fusion(f32[64,128,256]{2,1,0:T(8,128)} %broadcast_in_dim.40, s32[160]{0:T(256)S(1)} %bitcast.55, f32[160,128,256]{2,1,0:T(8,128)} %copy.31), kind=kCustom, calls=%fused_computation.1 | custom fusion | flops 5242880 | bytes 62915200 | tf_op jit(solution)/shard_map/scatter-add | solution.py:38
  94.0 5.9 convert_element_type.59
  99.9 0.0 reduce-scatter.4.cloned.1.call-update
  99.9 0.0 all-gather.2.cloned.1.call-start
  100.0 224.3 %reduce-scatter.4.cloned.1.call-done = bf16[2,128,256]{2,1,0:T(8,128)(2,1)} async-done(((bf16[64,128,256]{2,1,0:T(8,128)(2,1)}), bf16[2,128,256]{2,1,0:T(8,128)(2,1)}) %reduce-scatter.4.cloned.1.call-update) | async-done | bytes 131088 | tf_op jit(solution)/shard_map/reduce_scatter | solution.py:40
  324.2 0.8 slice.35
  325.1 1.3 collective-permute-done
  326.4 1.5 subtract_convert_fusion
  327.8 0.0 all-gather.2.cloned.1.call-update
  327.9 0.0 reduce-scatter.6.cloned.1.call-start
  327.9 0.7 copy.46
  328.6 75.5 %all-gather.2.cloned.1.call-done = bf16[32,128,256]{2,1,0:T(8,128)(2,1)} async-done(((bf16[1,128,256]{2,1,0:T(8,128)(2,1)}), bf16[32,128,256]{2,1,0:T(8,128)(2,1)}) %all-gather.2.cloned.1.call-update) | async-done | bytes 2097168 | tf_op jit(solution)/shard_map/all_gather | solution.py:46
  404.1 2.3 convolution_convert_fusion.1
  406.4 2.0 convert_bitcast_fusion.1
  408.5 0.0 reduce-scatter.6.cloned.1.call-update
  408.5 213.7 %reduce-scatter.6.cloned.1.call-done = bf16[1,128,256]{1,2,0:T(8,128)(2,1)} async-done(((bf16[32,128,256]{1,2,0:T(8,128)(2,1)}), bf16[1,128,256]{1,2,0:T(8,128)(2,1)}) %reduce-scatter.6.cloned.1.call-update) | async-done | bytes 65552 | tf_op jit(solution)/shard_map/reduce_scatter | solution.py:66
  622.2 0.9 copy.33
  623.2 1.6 stack.2
  624.7 7.0 all-to-all-start
  631.7 0.0 reduce-scatter.8.cloned.1.call-start
  631.8 0.6 constant_dynamic-slice_fusion
  634.4 0.7 and_reduce_fusion
  635.1 0.7 select_bitcast_fusion
  635.7 0.1 copy.38
  635.8 0.2 broadcast_in_dim.45
  636.1 1.3 copy-done.2
  637.4 0.0 reduce-scatter.8.cloned.1.call-update
  637.5 41.1 %all-to-all-done = bf16[32,1,128,256]{3,2,1,0:T(8,128)(2,1)} async-done(((bf16[32,1,128,256]{3,2,1,0:T(8,128)(2,1)}), bf16[32,1,128,256]{3,2,1,0:T(8,128)(2,1)}, u32[]{:S(2)}, u32[]{:S(2)}) %all-to-all-start) | async-done | bytes 2097184 | tf_op jit(solution)/shard_map/all_to_all | solution.py:76
  678.6 0.1 copy.34
  678.7 0.1 reshape.128
  678.8 0.8 copy.40
  679.5 3.5 collective-permute-done.1
  683.1 2.5 broadcast_select_fusion.2
  685.6 2.4 pad_maximum_fusion
  688.0 9.8 %gather_fusion = bf16[160,128,256]{2,1,0:T(8,128)(2,1)} fusion(bf16[64,128,256]{2,1,0:T(8,128)(2,1)} %pad_maximum_fusion, s32[1024]{0:T(1024)S(1)} %pad_clamp_fusion), kind=kCustom, calls=%fused_computation | custom fusion | bytes 20972160 | tf_op jit(solution)/shard_map/gather | solution.py:82
  697.8 14.8 %copy.35 = bf16[32,5,128,256]{2,3,1,0:T(8,128)(2,1)} copy(bf16[32,5,128,256]{3,2,1,0:T(8,128)(2,1)} %bitcast.50) | data formatting | bytes 20971520 | tf_op jit(solution)/shard_map/gather | solution.py:82
  712.6 9.2 %convert_bitcast_fusion = bf16[32,128,256]{1,2,0:T(8,128)(2,1)} fusion(bf16[32,128,128]{2,1,0:T(8,128)(2,1)S(1)} %copy-done.6, bf16[32,128,256]{2,1,0:T(8,128)(2,1)} %copy-done.3, bf16[32,5,128,128]{3,2,1,0:T(8,128)(2,1)} %param.12, bf16[32,5,128,256]{2,3,1,0:T(8,128)(2,1)} %copy.35, pred[32,5]{1,0:T(8,128)(4,1)S(1)} %iota_compare_fusion), kind=kOutput, calls=%fused_computation.11 | convolution fusion | flops 1620049920 | bytes 20971680 | tf_op jit(solution)/shard_map/kba,kbr->kar/dot_general | solution.py:86
  721.8 4.1 copy.39
  725.9 134.2 %reduce-scatter.8.cloned.1.call-done = bf16[1,128,256]{2,1,0:T(8,128)(2,1)} async-done(((bf16[32,128,256]{2,1,0:T(8,128)(2,1)}), bf16[1,128,256]{2,1,0:T(8,128)(2,1)}) %reduce-scatter.8.cloned.1.call-update) | async-done | bytes 65552 | tf_op jit(solution)/shard_map/reduce_scatter | solution.py:61
  (26 shorter events, 0.1 us)
Async XLA Ops:
  7.2 2.0 copy-start
  7.2 317.1 %reduce-scatter.4.cloned.1.call-start = ((), (), s32[]{:S(2)}) async-start(), calls=%async_computation.4 | async-start | bytes 4325376 | tf_op jit(solution)/shard_map/reduce_scatter | solution.py:40
  8.3 3.0 copy-start.4
  11.3 9.0 %copy-start.3 = (bf16[32,128,256]{2,1,0:T(8,128)(2,1)}, bf16[32,128,256]{2,1,0:T(8,128)(2,1)S(1)}, u32[]{:S(2)}) copy-start(bf16[32,128,256]{2,1,0:T(8,128)(2,1)S(1)} %convolution_convert_fusion) | copy-start | bytes 6291460
  99.9 226.4 %copy-start.8 = (bf16[1,128,256]{2,1,0:T(8,128)(2,1)S(1)}, bf16[1,128,256]{2,1,0:T(8,128)(2,1)}, u32[]{:S(2)}) copy-start(bf16[1,128,256]{2,1,0:T(8,128)(2,1)} %param.15) | copy-start | bytes 196612
  99.9 228.0 %copy-start.5 = (bf16[1,128,4096]{2,1,0:T(8,128)(2,1)S(1)}, bf16[1,128,4096]{2,1,0:T(8,128)(2,1)}, u32[]{:S(2)}) copy-start(bf16[1,128,4096]{2,1,0:T(8,128)(2,1)} %param.17) | copy-start | bytes 3145732
  99.9 304.1 %all-gather.2.cloned.1.call-start = ((), (), s32[]{:S(2)}) async-start(), calls=%async_computation.5 | async-start | bytes 2162688 | tf_op jit(solution)/shard_map/all_gather | solution.py:46
  325.1 1.3 collective-permute-start
  327.9 294.3 %reduce-scatter.6.cloned.1.call-start = ((), (), s32[]{:S(2)}) async-start(), calls=%async_computation.6 | async-start | bytes 2162688 | tf_op jit(solution)/shard_map/reduce_scatter | solution.py:66
  408.5 223.3 %copy-start.10 = (s32[1,32]{1,0:T(1,128)S(1)}, s32[1,32]{1,0:T(1,128)}, u32[]{:S(2)}) copy-start(s32[1,32]{1,0:T(1,128)} %param.16) | copy-start | bytes 388
  408.5 225.9 %copy-start.9 = (s32[3]{0:T(128)S(1)}, s32[3]{0:T(128)}, u32[]{:S(2)}) copy-start(s32[3]{0:T(128)} %constant.102.clone.1) | copy-start | bytes 40
  624.7 54.1 %copy-start.7 = (bf16[1,128,256]{1,2,0:T(8,128)(2,1)S(1)}, bf16[1,128,256]{1,2,0:T(8,128)(2,1)}, u32[]{:S(2)}) copy-start(bf16[1,128,256]{1,2,0:T(8,128)(2,1)} %reduce-scatter.6.cloned.1.call-done) | copy-start | bytes 196612
  624.7 53.8 %all-to-all-start = ((bf16[32,1,128,256]{3,2,1,0:T(8,128)(2,1)}), bf16[32,1,128,256]{3,2,1,0:T(8,128)(2,1)}, u32[]{:S(2)}, u32[]{:S(2)}) async-start(bf16[32,1,128,256]{3,2,1,0:T(8,128)(2,1)} %stack.2), calls=%async_computation.2 | async-start | bytes 4194304 | tf_op jit(solution)/shard_map/all_to_all | solution.py:76
  631.7 228.3 %reduce-scatter.8.cloned.1.call-start = ((), (), s32[]{:S(2)}) async-start(), calls=%async_computation.7 | async-start | bytes 2162688 | tf_op jit(solution)/shard_map/reduce_scatter | solution.py:61
  636.1 1.3 copy-start.2
  678.6 4.5 collective-permute-start.1
  697.8 14.8 %copy-start.6 = (bf16[32,128,128]{2,1,0:T(8,128)(2,1)S(1)}, bf16[32,128,128]{2,1,0:T(8,128)(2,1)}, u32[]{:S(2)}) copy-start(bf16[32,128,128]{2,1,0:T(8,128)(2,1)} %param.10) | copy-start | bytes 3145732
  712.6 147.5 %copy-start.1 = (bf16[32,128,256]{2,1,0:T(8,128)(2,1)S(1)}, bf16[32,128,256]{2,1,0:T(8,128)(2,1)}, u32[]{:S(2)}) copy-start(bf16[32,128,256]{2,1,0:T(8,128)(2,1)} %param.11) | copy-start | bytes 6291460
Sparse Core Ops, SparseCore 0:
  100.1 224.1 reduce-scatter.3
  328.0 76.0 all-gather.1
  408.6 213.5 reduce-scatter.5
  637.6 222.4 reduce-scatter.7
